TPU v7x, 512 devices: a whole 4x8x8 slice. The times are simulated.
512 devices in a mesh: batch: 32 (over z, x), blk: 16 (over y, core).
Axes of the slice: x: 4, y: 8, z: 8, core: 2. Of those that a mesh axis runs over, the one named last changes fastest.
Arguments:
- points: float32 [1024, 16, 3, 256], P('batch', 'blk'), may hold values from -6 to 6
- centers: float32 [1024, 16, 3, 384], P('batch', 'blk'), may hold values from -6 to 6
- exponents: float32 [1024, 16, 384], P('batch', 'blk'), may hold values from 0.1 to 1
- angular: float32 [1024, 16, 3, 384], P('batch', 'blk'), may hold values from -3 to 3
- grid_weights: float32 [1024, 16, 256], P('batch', 'blk'), may hold values from 0.001 to 0.01
- hartree: float32 [1024, 16, 256], P('batch', 'blk'), may hold values from 0 to 1.7
- load_plan: int32 [16, 1024], P('blk'), may hold values from 0 to 1023, each once within a row
- density_blocks: bfloat16 [256, 128, 128], P('blk'), may hold values from -0.046875 to 0.046875
- pair_lists: int32 [32, 16, 16, 2], P('batch', 'blk'), may hold values from 0 to 15
- batch_pairs: int32 [1024, 16, 9], P('batch', 'blk'), may hold values from 0 to 31, as said below
Outputs:
- hamiltonian: float32 [256, 128, 128], P('blk')
- density: float32 [1024, 16, 256], P('batch', 'blk')
Inputs may be any that keep to these rules, and one draw needn't show every extreme that they name: Each row of load_plan names every storage row of its column once. `pair_lists`: local index of a block pair within the 16 pairs held by one index of blk. `batch_pairs`: entry e of a device's table is the (e % 2)-th block it reads from index e // 2 of blk; every entry of a device's table is named by some pair of its batches.
All inputs are finite; a program needn't handle non-finite values.
Results may differ from a plain program's by a relative error of at most 0.0065.
Values may be sent and summed in bfloat16 or wider, within the bound.
No kernel may reach another device: no remote copies, remote signals or barrier semaphores. Data moves between devices by JAX's collectives and lax.ppermute only.
A program may use at most 64 MiB of HBM per device.

v0:
```python
import jax
import jax.numpy as jnp
from jax import lax
from jax.sharding import PartitionSpec as P

LIST = 3
xc_scale = 0.98474502
soft_square = 0.01


def exchange_potential(grid_rho):
    return -xc_scale * jnp.power(grid_rho * grid_rho + soft_square, 1.0 / 6.0)


def evaluate(points, centers, exponents, angular):
    distance = jnp.zeros(points.shape[:-2] + (points.shape[-1], centers.shape[-1]), jnp.float32)
    angular_part = jnp.ones_like(distance)
    for component in range(3):
        delta = points[..., component, :, None] - centers[..., component, None, :]
        distance = distance + delta * delta
        angular_part = angular_part + angular[..., component, None, :] * delta
    return (jnp.exp(-exponents[..., None, :] * distance) * angular_part).astype(jnp.bfloat16)


def on_device(
    points,
    centers,
    exponents,
    angular,
    grid_weights,
    hartree,
    load_plan,
    density_blocks,
    pair_lists,
    batch_pairs,
):
    slot_count = points.shape[0]
    grid_size = points.shape[3]
    columns = lax.axis_size("blk")
    per_owner = pair_lists.shape[3]
    held_pairs = density_blocks.shape[0]
    block_size = density_blocks.shape[1]
    entries = columns * per_owner
    list_size = LIST
    basis_width = list_size * block_size
    batch_rank = lax.axis_index("batch")
    plan_rows = lax.dynamic_slice_in_dim(load_plan[0], batch_rank * slot_count, slot_count)
    stored = lax.all_gather(hartree[:, 0, :], "batch", axis=0, tiled=True)
    potential = stored[plan_rows]
    wanted = pair_lists[0, 0]
    asked_slots = lax.all_to_all(wanted, "blk", split_axis=0, concat_axis=0, tiled=True)
    owner_base = jnp.arange(entries, dtype=jnp.int32) // per_owner * held_pairs
    global_ids = owner_base + wanted.reshape(entries)
    blank_table = jnp.zeros((entries, block_size, block_size), jnp.bfloat16)
    piece = lax.all_gather(density_blocks, "blk", axis=0, tiled=True)
    inside = (global_ids >= 0) & (global_ids < piece.shape[0])
    chosen = piece[jnp.clip(global_ids, 0, piece.shape[0] - 1)]
    fetched = jnp.where(inside[:, None, None], chosen, blank_table)
    group_size = 4
    loop_turns = slot_count // group_size

    def take_rows(value, turn_index):
        return lax.dynamic_slice_in_dim(value, turn_index * group_size, group_size, 0)

    def integrate(partial_table, turn_index):
        basis = evaluate(
            take_rows(points, turn_index)[:, 0],
            take_rows(centers, turn_index)[:, 0],
            take_rows(exponents, turn_index)[:, 0],
            take_rows(angular, turn_index)[:, 0],
        )
        slot_refs = take_rows(batch_pairs, turn_index)[:, 0]
        blocks = fetched[slot_refs]
        sub_density = (
            blocks.reshape(group_size, list_size, list_size, block_size, block_size)
            .transpose(0, 1, 3, 2, 4)
            .reshape(group_size, basis_width, basis_width)
        )
        inner = jnp.einsum("gpm,gmn->gpn", basis, sub_density, preferred_element_type=jnp.float32)
        grid_rho = jnp.sum(inner * basis.astype(jnp.float32), axis=-1)
        effective = take_rows(potential, turn_index) + exchange_potential(grid_rho)
        weight_rows = take_rows(grid_weights, turn_index)[:, 0]
        scaled = ((weight_rows * effective)[..., None] * basis.astype(jnp.float32)).astype(
            jnp.bfloat16
        )
        full_blocks = jnp.einsum("gpm,gpn->gmn", basis, scaled, preferred_element_type=jnp.float32)
        contributions = (
            full_blocks.reshape(group_size, list_size, block_size, list_size, block_size)
            .transpose(0, 1, 3, 2, 4)
            .reshape(group_size * list_size * list_size, block_size, block_size)
        )
        partial_table = partial_table.at[slot_refs.reshape(-1)].add(contributions)
        return (partial_table, grid_rho)

    zero_table = jnp.zeros((entries, block_size, block_size), jnp.float32)
    partial_table, rho_groups = lax.scan(integrate, zero_table, jnp.arange(loop_turns))
    grid_rho = rho_groups.reshape(slot_count, grid_size)
    received = lax.all_to_all(
        partial_table.reshape(columns, per_owner, block_size, block_size),
        "blk",
        split_axis=0,
        concat_axis=0,
        tiled=True,
    )
    owned_sums = (
        jnp.zeros((held_pairs, block_size, block_size), jnp.float32)
        .at[asked_slots.reshape(entries)]
        .add(received.reshape(entries, block_size, block_size))
    )
    hamiltonian = lax.psum(owned_sums, "batch")
    batch_total = load_plan.shape[1]
    placement = (plan_rows[None, :] == jnp.arange(batch_total, dtype=jnp.int32)[:, None]).astype(
        jnp.float32
    )
    spread_rows = jnp.dot(
        placement, grid_rho, precision=lax.Precision.HIGHEST, preferred_element_type=jnp.float32
    )
    density = lax.psum_scatter(spread_rows, "batch", scatter_dimension=0, tiled=True)
    return (hamiltonian, density[:, None, :])


def solution(mesh):
    return jax.shard_map(
        on_device,
        mesh=mesh,
        in_specs=(
            P("batch", "blk", None, None),
            P("batch", "blk", None, None),
            P("batch", "blk", None),
            P("batch", "blk", None, None),
            P("batch", "blk", None),
            P("batch", "blk", None),
            P("blk", None),
            P("blk", None, None),
            P("batch", "blk", None, None),
            P("batch", "blk", None),
        ),
        out_specs=(P("blk", None, None), P("batch", "blk", None)),
        check_vma=False,
    )
```

profile of v0, /device:TPU:8, one launch (start us, length us, event | category | flops | bytes accessed | tf_op | source)
XLA Modules:
  0.0 800.7 jit_solution(2311108223574678586)
XLA Ops:
  7.2 1.4 copy.57
  9.4 1.3 copy.56
  10.7 9.1 %all-to-all-start = ((s32[16,1,2]{2,1,0:T(1,128)}), s32[16,1,2]{2,1,0:T(1,128)S(1)}, u32[]{:S(2)}, u32[]{:S(2)}) async-start(s32[16,1,2]{2,1,0:T(1,128)} %copy.56), calls=%async_computation | async-start | bytes 16384 | tf_op jit(solution)/shard_map/all_to_all | solution.py:51
  22.3 76.3 %all-gather.6.cloned.1.call-done = f32[1024,1,256]{2,0,1:T(8,128)} async-done(((f32[32,1,256]{2,0,1:T(8,128)}), f32[1024,1,256]{2,0,1:T(8,128)}) %all-gather.6.cloned.1.call-update) | async-done | bytes 1048592 | tf_op jit(solution)/shard_map/all_gather | solution.py:48
  98.6 1.8 gather_fusion.1
  100.4 54.4 %all-gather.4.cloned.1.call-done = bf16[256,128,128]{2,1,0:T(8,128)(2,1)} async-done(((bf16[16,128,128]{2,1,0:T(8,128)(2,1)}), bf16[256,128,128]{2,1,0:T(8,128)(2,1)}) %all-gather.4.cloned.1.call-update) | async-done | bytes 8388624 | tf_op jit(solution)/shard_map/all_gather | solution.py:55
  154.8 4.1 gather_fusion.2
  159.1 1.5 broadcast_in_dim.40
  160.6 234.9 %while.12 = (s32[]{:T(128)}, f32[32,128,128]{2,1,0:T(8,128)}, f32[8,4,256]{2,1,0:T(4,128)S(1)}, s32[8]{0:T(128)S(1)}, s32[32,1,9]{2,0,1:T(8,128)S(1)}, /*index=5...) while((s32[]{:T(128)}, f32[32,128,128]{2,1,0:T(8,128)}, ...), condition=%wide.region_3.4_spmd, body=%wide.region_0.3_spmd.sunk | while | flops 633674496 | bytes 35997664 | solution.py:96
  165.4 1.1 reshape.301
  167.2 2.9 fusion.49
  170.8 4.2 fusion.51
  175.1 3.5 reshape.302
  178.5 1.7 copy.100
  180.3 9.6 %scatter_fusion = f32[32,128,128]{2,1,0:T(8,128)} fusion(f32[32,128,128]{2,1,0:T(8,128)} %get-tuple-element.276, s32[36]{0:T(128)S(1)} %fusion.47, f32[36,128,128]{2,1,0:T(8,128)} %bitcast.106), kind=kCustom, calls=%fused_computation.3.clone.1 | custom fusion | flops 589824 | bytes 7078032 | tf_op jit(solution)/shard_map/while/body/eval_jaxpr/scatter-add | solution.py:92
  194.8 1.1 reshape.301
  196.6 2.9 fusion.49
  200.2 4.2 fusion.51
  204.4 3.5 reshape.302
  207.9 1.7 copy.100
  209.7 9.7 %scatter_fusion = f32[32,128,128]{2,1,0:T(8,128)} fusion(f32[32,128,128]{2,1,0:T(8,128)} %get-tuple-element.276, s32[36]{0:T(128)S(1)} %fusion.47, f32[36,128,128]{2,1,0:T(8,128)} %bitcast.106), kind=kCustom, calls=%fused_computation.3.clone.1 | custom fusion | flops 589824 | bytes 7078032 | tf_op jit(solution)/shard_map/while/body/eval_jaxpr/scatter-add | solution.py:92
  224.2 1.1 reshape.301
  226.0 2.9 fusion.49
  229.6 4.2 fusion.51
  233.8 3.5 reshape.302
  237.3 1.7 copy.100
  239.1 9.7 %scatter_fusion = f32[32,128,128]{2,1,0:T(8,128)} fusion(f32[32,128,128]{2,1,0:T(8,128)} %get-tuple-element.276, s32[36]{0:T(128)S(1)} %fusion.47, f32[36,128,128]{2,1,0:T(8,128)} %bitcast.106), kind=kCustom, calls=%fused_computation.3.clone.1 | custom fusion | flops 589824 | bytes 7078032 | tf_op jit(solution)/shard_map/while/body/eval_jaxpr/scatter-add | solution.py:92
  253.6 1.1 reshape.301
  255.4 2.9 fusion.49
  259.0 4.2 fusion.51
  263.2 3.5 reshape.302
  266.7 1.7 copy.100
  268.5 9.7 %scatter_fusion = f32[32,128,128]{2,1,0:T(8,128)} fusion(f32[32,128,128]{2,1,0:T(8,128)} %get-tuple-element.276, s32[36]{0:T(128)S(1)} %fusion.47, f32[36,128,128]{2,1,0:T(8,128)} %bitcast.106), kind=kCustom, calls=%fused_computation.3.clone.1 | custom fusion | flops 589824 | bytes 7078032 | tf_op jit(solution)/shard_map/while/body/eval_jaxpr/scatter-add | solution.py:92
  283.0 1.1 reshape.301
  284.8 2.9 fusion.49
  288.4 4.2 fusion.51
  292.6 3.5 reshape.302
  296.1 1.7 copy.100
  297.9 9.7 %scatter_fusion = f32[32,128,128]{2,1,0:T(8,128)} fusion(f32[32,128,128]{2,1,0:T(8,128)} %get-tuple-element.276, s32[36]{0:T(128)S(1)} %fusion.47, f32[36,128,128]{2,1,0:T(8,128)} %bitcast.106), kind=kCustom, calls=%fused_computation.3.clone.1 | custom fusion | flops 589824 | bytes 7078032 | tf_op jit(solution)/shard_map/while/body/eval_jaxpr/scatter-add | solution.py:92
  312.4 1.1 reshape.301
  314.2 2.9 fusion.49
  317.8 4.2 fusion.51
  322.0 3.5 reshape.302
  325.5 1.7 copy.100
  327.3 9.6 %scatter_fusion = f32[32,128,128]{2,1,0:T(8,128)} fusion(f32[32,128,128]{2,1,0:T(8,128)} %get-tuple-element.276, s32[36]{0:T(128)S(1)} %fusion.47, f32[36,128,128]{2,1,0:T(8,128)} %bitcast.106), kind=kCustom, calls=%fused_computation.3.clone.1 | custom fusion | flops 589824 | bytes 7078032 | tf_op jit(solution)/shard_map/while/body/eval_jaxpr/scatter-add | solution.py:92
  343.5 2.9 fusion.49
  347.1 4.2 fusion.51
  351.3 3.5 reshape.302
  354.8 1.7 copy.100
  356.6 9.6 %scatter_fusion = f32[32,128,128]{2,1,0:T(8,128)} fusion(f32[32,128,128]{2,1,0:T(8,128)} %get-tuple-element.276, s32[36]{0:T(128)S(1)} %fusion.47, f32[36,128,128]{2,1,0:T(8,128)} %bitcast.106), kind=kCustom, calls=%fused_computation.3.clone.1 | custom fusion | flops 589824 | bytes 7078032 | tf_op jit(solution)/shard_map/while/body/eval_jaxpr/scatter-add | solution.py:92
  371.1 1.1 reshape.301
  372.8 2.9 fusion.49
  376.5 4.2 fusion.51
  380.7 3.5 reshape.302
  384.2 1.7 copy.100
  386.0 9.6 %scatter_fusion = f32[32,128,128]{2,1,0:T(8,128)} fusion(f32[32,128,128]{2,1,0:T(8,128)} %get-tuple-element.276, s32[36]{0:T(128)S(1)} %fusion.47, f32[36,128,128]{2,1,0:T(8,128)} %bitcast.106), kind=kCustom, calls=%fused_computation.3.clone.1 | custom fusion | flops 589824 | bytes 7078032 | tf_op jit(solution)/shard_map/while/body/eval_jaxpr/scatter-add | solution.py:92
  395.5 6.8 all-to-all-start.1
  403.2 1.5 fusion.21
  406.1 43.7 %all-to-all-done.1 = f32[16,2,128,128]{3,2,1,0:T(8,128)S(1)} async-done(((f32[16,2,128,128]{3,2,1,0:T(8,128)}), f32[16,2,128,128]{3,2,1,0:T(8,128)S(1)}, u32[]{:S(2)}, u32[]{:S(2)}) %all-to-all-start.1) | async-done | bytes 2097184 | tf_op jit(solution)/shard_map/all_to_all | solution.py:98
  449.9 2.7 scatter_fusion.1
  453.5 175.6 %reduce-scatter.2.cloned.1.call-done = f32[32,256]{1,0:T(8,128)} async-done(((f32[1024,256]{1,0:T(8,128)}), f32[32,256]{1,0:T(8,128)}) %reduce-scatter.2.cloned.1.call-update) | async-done | bytes 32784 | tf_op jit(solution)/shard_map/reduce_scatter | solution.py:118
  629.1 1.4 copy.66
  630.5 161.3 %all-reduce.2.cloned.1.call-done = f32[16,128,128]{2,1,0:T(8,128)} async-done(((f32[16,128,128]{2,1,0:T(8,128)}), f32[16,128,128]{2,1,0:T(8,128)}) %all-reduce.2.cloned.1.call-update) | async-done | bytes 1048592 | tf_op jit(solution)/shard_map/psum | solution.py:110
  791.8 2.3 copy.114
  (231 shorter events, 52.5 us)
Async XLA Ops:
  7.2 91.4 %all-gather.6.cloned.1.call-start = ((), (), s32[]{:S(2)}) async-start(), calls=%async_computation.6 | async-start | bytes 1081344 | tf_op jit(solution)/shard_map/all_gather | solution.py:48
  8.6 146.2 %all-gather.4.cloned.1.call-start = ((), (), s32[]{:S(2)}) async-start(), calls=%async_computation.3 | async-start | bytes 8912896 | tf_op jit(solution)/shard_map/all_gather | solution.py:55
  10.7 384.8 %all-to-all-start = ((s32[16,1,2]{2,1,0:T(1,128)}), s32[16,1,2]{2,1,0:T(1,128)S(1)}, u32[]{:S(2)}, u32[]{:S(2)}) async-start(s32[16,1,2]{2,1,0:T(1,128)} %copy.56), calls=%async_computation | async-start | bytes 16384 | tf_op jit(solution)/shard_map/all_to_all | solution.py:51
  160.6 3.8 copy-start
  180.3 9.6 %copy-start.1 = (bf16[32,128,128]{2,1,0:T(8,128)(2,1)S(1)}, bf16[32,128,128]{2,1,0:T(8,128)(2,1)}, u32[]{:S(2)}) copy-start(bf16[32,128,128]{2,1,0:T(8,128)(2,1)} %copy-done) | copy-start | bytes 3145732 | tf_op jit(solution)/shard_map/while
  190.0 3.8 copy-start
  209.7 9.7 %copy-start.1 = (bf16[32,128,128]{2,1,0:T(8,128)(2,1)S(1)}, bf16[32,128,128]{2,1,0:T(8,128)(2,1)}, u32[]{:S(2)}) copy-start(bf16[32,128,128]{2,1,0:T(8,128)(2,1)} %copy-done) | copy-start | bytes 3145732 | tf_op jit(solution)/shard_map/while
  219.4 3.8 copy-start
  239.1 9.7 %copy-start.1 = (bf16[32,128,128]{2,1,0:T(8,128)(2,1)S(1)}, bf16[32,128,128]{2,1,0:T(8,128)(2,1)}, u32[]{:S(2)}) copy-start(bf16[32,128,128]{2,1,0:T(8,128)(2,1)} %copy-done) | copy-start | bytes 3145732 | tf_op jit(solution)/shard_map/while
  248.8 3.8 copy-start
  268.5 9.8 %copy-start.1 = (bf16[32,128,128]{2,1,0:T(8,128)(2,1)S(1)}, bf16[32,128,128]{2,1,0:T(8,128)(2,1)}, u32[]{:S(2)}) copy-start(bf16[32,128,128]{2,1,0:T(8,128)(2,1)} %copy-done) | copy-start | bytes 3145732 | tf_op jit(solution)/shard_map/while
  278.2 3.8 copy-start
  297.9 9.7 %copy-start.1 = (bf16[32,128,128]{2,1,0:T(8,128)(2,1)S(1)}, bf16[32,128,128]{2,1,0:T(8,128)(2,1)}, u32[]{:S(2)}) copy-start(bf16[32,128,128]{2,1,0:T(8,128)(2,1)} %copy-done) | copy-start | bytes 3145732 | tf_op jit(solution)/shard_map/while
  307.6 3.8 copy-start
  327.3 9.6 %copy-start.1 = (bf16[32,128,128]{2,1,0:T(8,128)(2,1)S(1)}, bf16[32,128,128]{2,1,0:T(8,128)(2,1)}, u32[]{:S(2)}) copy-start(bf16[32,128,128]{2,1,0:T(8,128)(2,1)} %copy-done) | copy-start | bytes 3145732 | tf_op jit(solution)/shard_map/while
  336.9 3.8 copy-start
  356.6 9.6 %copy-start.1 = (bf16[32,128,128]{2,1,0:T(8,128)(2,1)S(1)}, bf16[32,128,128]{2,1,0:T(8,128)(2,1)}, u32[]{:S(2)}) copy-start(bf16[32,128,128]{2,1,0:T(8,128)(2,1)} %copy-done) | copy-start | bytes 3145732 | tf_op jit(solution)/shard_map/while
  366.3 3.8 copy-start
  386.0 9.6 %copy-start.1 = (bf16[32,128,128]{2,1,0:T(8,128)(2,1)S(1)}, bf16[32,128,128]{2,1,0:T(8,128)(2,1)}, u32[]{:S(2)}) copy-start(bf16[32,128,128]{2,1,0:T(8,128)(2,1)} %copy-done) | copy-start | bytes 3145732 | tf_op jit(solution)/shard_map/while
  395.5 54.2 %all-to-all-start.1 = ((f32[16,2,128,128]{3,2,1,0:T(8,128)}), f32[16,2,128,128]{3,2,1,0:T(8,128)S(1)}, u32[]{:S(2)}, u32[]{:S(2)}) async-start(f32[16,2,128,128]{3,2,1,0:T(8,128)} %bitcast.108), calls=%async_computation.1 | async-start | bytes 4194304 | tf_op jit(solution)/shard_map/all_to_all | solution.py:98
  402.4 226.8 %reduce-scatter.2.cloned.1.call-start = ((), (), s32[]{:S(2)}) async-start(), calls=%async_computation.5 | async-start | bytes 1081344 | tf_op jit(solution)/shard_map/reduce_scatter | solution.py:118
  404.7 387.1 %all-reduce.2.cloned.1.call-start = ((), (), s32[]{:S(2)}) async-start(), calls=%async_computation.4 | async-start | bytes 2097152 | tf_op jit(solution)/shard_map/psum | solution.py:110
  452.5 1.0 copy-start.2
Sparse Core Ops, SparseCore 0:
  11.7 86.7 all-gather.5
  100.7 54.0 all-gather.3
  407.6 221.4 reduce-scatter.1
  633.0 158.7 all-reduce.1
where the time goes:
time: 804 us; the launch traced here: 801 us
  waiting for transfers between devices  512 us (64%)
  local copies, waits for them, and re-layouts  112 us (14%)
  other arithmetic  81.9 us (10%)
  matrix products  58.4 us (7%)
  starting transfers between devices  16.1 us (2%)
  between operations  13.9 us (2%)
    reduce_scatter x1, waiting for transfers between devices, on_device(): lax.psum_scatter(spread_rows, 'batch', scatter_dimension=0, tiled=True)  176 us
    psum x1, waiting for transfers between devices, on_device(): hamiltonian = lax.psum(owned_sums, 'batch')  161 us
    scatter-add x8, other arithmetic, integrate(): partial_table = partial_table.at[slot_refs.reshape(-1)].add(contributions)  77.2 us
    all_gather x1, waiting for transfers between devices, on_device(): stored = lax.all_gather(hartree[:, 0, :], 'batch', axis=0, tiled=True)  76.3 us
    all_gather x1, waiting for transfers between devices, on_device(): piece = lax.all_gather(density_blocks, 'blk', axis=0, tiled=True)  54.4 us
    all_to_all x1, waiting for transfers between devices, on_device(): lax.all_to_all(partial_table.reshape(columns, per_owner, block_size, bloc...  43.7 us
    dot_general x8, matrix products, integrate(): jnp.einsum('gpm,gpn->gmn', basis, scaled, preferred_element_type=jnp.floa...  33.7 us
    reshape x8, local copies, waits for them, and re-layouts, integrate(): full_blocks.reshape(group_size, list_size, block_size, list_size, block_s...  27.7 us
  transfers between devices with their start and end apart: 6, of which 5 were waited for; matrix products, arithmetic and copies ran while one was open for 31% of the time, Pallas kernels for 0%

commit v1 on v0

--- a/solution.py
+++ b/solution.py
@@ -6,6 +6,12 @@
 LIST = 3
 xc_scale = 0.98474502
 soft_square = 0.01
+
+
+def gather_and_add(x, mesh_axis):
+    parts = lax.all_gather(x, mesh_axis, axis=0, tiled=False)
+    acc = parts.sum(axis=0)
+    return acc
 
 
 def exchange_potential(grid_rho):
@@ -107,7 +113,7 @@
         .at[asked_slots.reshape(entries)]
         .add(received.reshape(entries, block_size, block_size))
     )
-    hamiltonian = lax.psum(owned_sums, "batch")
+    hamiltonian = gather_and_add(owned_sums, "batch")
     batch_total = load_plan.shape[1]
     placement = (plan_rows[None, :] == jnp.arange(batch_total, dtype=jnp.int32)[:, None]).astype(
         jnp.float32

time: 804 us -> 893 us (1.11)
  the two profiles are of different devices: /device:TPU:8 before, /device:TPU:1 now
where the time goes in v1:
time: 893 us; the launch traced here: 890 us
  waiting for transfers between devices  592 us (66%)
  local copies, waits for them, and re-layouts  110 us (12%)
  other arithmetic  94.8 us (11%)
  matrix products  58.4 us (7%)
  starting transfers between devices  15.2 us (2%)
  between operations  13.9 us (2%)
    all_gather x1, waiting for transfers between devices, gather_and_add(): parts = lax.all_gather(x, mesh_axis, axis=0, tiled=False)  244 us
    reduce_scatter x1, waiting for transfers between devices, on_device(): lax.psum_scatter(spread_rows, 'batch', scatter_dimension=0, tiled=True)  169 us
    scatter-add x8, other arithmetic, integrate(): partial_table = partial_table.at[slot_refs.reshape(-1)].add(contributions)  77.4 us
    all_gather x1, waiting for transfers between devices, on_device(): stored = lax.all_gather(hartree[:, 0, :], 'batch', axis=0, tiled=True)  71.7 us
    all_gather x1, waiting for transfers between devices, on_device(): piece = lax.all_gather(density_blocks, 'blk', axis=0, tiled=True)  60.7 us
    all_to_all x1, waiting for transfers between devices, on_device(): lax.all_to_all(partial_table.reshape(columns, per_owner, block_size, bloc...  45.3 us
    dot_general x8, matrix products, integrate(): jnp.einsum('gpm,gpn->gmn', basis, scaled, preferred_element_type=jnp.floa...  33.7 us
    reshape x8, local copies, waits for them, and re-layouts, integrate(): full_blocks.reshape(group_size, list_size, block_size, list_size, block_s...  27.7 us
  transfers between devices with their start and end apart: 6, of which 5 were waited for; matrix products, arithmetic and copies ran while one was open for 28% of the time, Pallas kernels for 0%

profile of v1, /device:TPU:1, one launch (start us, length us, event | category | flops | bytes accessed | tf_op | source)
XLA Modules:
  0.0 889.9 jit_solution(10053402453071526069)
XLA Ops:
  7.2 1.4 copy.57
  9.4 1.3 copy.56
  10.7 10.2 %all-to-all-start = ((s32[16,1,2]{2,1,0:T(1,128)}), s32[16,1,2]{2,1,0:T(1,128)S(1)}, u32[]{:S(2)}, u32[]{:S(2)}) async-start(s32[16,1,2]{2,1,0:T(1,128)} %copy.56), calls=%async_computation | async-start | bytes 16384 | tf_op jit(solution)/shard_map/all_to_all | solution.py:57
  23.4 71.7 %all-gather.8.cloned.1.call-done = f32[1024,1,256]{2,0,1:T(8,128)} async-done(((f32[32,1,256]{2,0,1:T(8,128)}), f32[1024,1,256]{2,0,1:T(8,128)}) %all-gather.8.cloned.1.call-update) | async-done | bytes 1048592 | tf_op jit(solution)/shard_map/all_gather | solution.py:54
  95.1 1.8 gather_fusion.1
  96.9 60.7 %all-gather.6.cloned.1.call-done = bf16[256,128,128]{2,1,0:T(8,128)(2,1)} async-done(((bf16[16,128,128]{2,1,0:T(8,128)(2,1)}), bf16[256,128,128]{2,1,0:T(8,128)(2,1)}) %all-gather.6.cloned.1.call-update) | async-done | bytes 8388624 | tf_op jit(solution)/shard_map/all_gather | solution.py:61
  157.6 4.1 gather_fusion.2
  161.9 1.5 broadcast_in_dim.40
  163.4 235.1 %while.12 = (s32[]{:T(128)}, f32[32,128,128]{2,1,0:T(8,128)}, f32[8,4,256]{2,1,0:T(4,128)S(1)}, s32[8]{0:T(128)S(1)}, s32[32,1,9]{2,0,1:T(8,128)S(1)}, /*index=5...) while((s32[]{:T(128)}, f32[32,128,128]{2,1,0:T(8,128)}, ...), condition=%wide.region_3.4_spmd, body=%wide.region_0.3_spmd.sunk | while | flops 633674496 | bytes 35997664 | solution.py:102
  168.2 1.1 reshape.302
  170.0 2.9 fusion.49
  173.6 4.2 fusion.51
  177.8 3.5 reshape.303
  181.3 1.7 copy.100
  183.1 9.7 %scatter_fusion = f32[32,128,128]{2,1,0:T(8,128)} fusion(f32[32,128,128]{2,1,0:T(8,128)} %get-tuple-element.276, s32[36]{0:T(128)S(1)} %fusion.47, f32[36,128,128]{2,1,0:T(8,128)} %bitcast.107), kind=kCustom, calls=%fused_computation.3.clone.1 | custom fusion | flops 589824 | bytes 7078032 | tf_op jit(solution)/shard_map/while/body/eval_jaxpr/scatter-add | solution.py:98
  197.6 1.1 reshape.302
  199.4 2.9 fusion.49
  203.0 4.2 fusion.51
  207.3 3.5 reshape.303
  210.7 1.7 copy.100
  212.5 9.7 %scatter_fusion = f32[32,128,128]{2,1,0:T(8,128)} fusion(f32[32,128,128]{2,1,0:T(8,128)} %get-tuple-element.276, s32[36]{0:T(128)S(1)} %fusion.47, f32[36,128,128]{2,1,0:T(8,128)} %bitcast.107), kind=kCustom, calls=%fused_computation.3.clone.1 | custom fusion | flops 589824 | bytes 7078032 | tf_op jit(solution)/shard_map/while/body/eval_jaxpr/scatter-add | solution.py:98
  227.0 1.1 reshape.302
  228.8 2.9 fusion.49
  232.4 4.2 fusion.51
  236.7 3.5 reshape.303
  240.1 1.7 copy.100
  241.9 9.7 %scatter_fusion = f32[32,128,128]{2,1,0:T(8,128)} fusion(f32[32,128,128]{2,1,0:T(8,128)} %get-tuple-element.276, s32[36]{0:T(128)S(1)} %fusion.47, f32[36,128,128]{2,1,0:T(8,128)} %bitcast.107), kind=kCustom, calls=%fused_computation.3.clone.1 | custom fusion | flops 589824 | bytes 7078032 | tf_op jit(solution)/shard_map/while/body/eval_jaxpr/scatter-add | solution.py:98
  256.5 1.1 reshape.302
  258.2 2.9 fusion.49
  261.9 4.2 fusion.51
  266.1 3.5 reshape.303
  269.6 1.7 copy.100
  271.4 9.6 %scatter_fusion = f32[32,128,128]{2,1,0:T(8,128)} fusion(f32[32,128,128]{2,1,0:T(8,128)} %get-tuple-element.276, s32[36]{0:T(128)S(1)} %fusion.47, f32[36,128,128]{2,1,0:T(8,128)} %bitcast.107), kind=kCustom, calls=%fused_computation.3.clone.1 | custom fusion | flops 589824 | bytes 7078032 | tf_op jit(solution)/shard_map/while/body/eval_jaxpr/scatter-add | solution.py:98
  285.8 1.1 reshape.302
  287.6 2.9 fusion.49
  291.2 4.2 fusion.51
  295.4 3.5 reshape.303
  298.9 1.7 copy.100
  300.7 9.6 %scatter_fusion = f32[32,128,128]{2,1,0:T(8,128)} fusion(f32[32,128,128]{2,1,0:T(8,128)} %get-tuple-element.276, s32[36]{0:T(128)S(1)} %fusion.47, f32[36,128,128]{2,1,0:T(8,128)} %bitcast.107), kind=kCustom, calls=%fused_computation.3.clone.1 | custom fusion | flops 589824 | bytes 7078032 | tf_op jit(solution)/shard_map/while/body/eval_jaxpr/scatter-add | solution.py:98
  315.1 1.1 reshape.302
  316.9 2.9 fusion.49
  320.5 4.2 fusion.51
  324.8 3.5 reshape.303
  328.2 1.7 copy.100
  330.0 9.7 %scatter_fusion = f32[32,128,128]{2,1,0:T(8,128)} fusion(f32[32,128,128]{2,1,0:T(8,128)} %get-tuple-element.276, s32[36]{0:T(128)S(1)} %fusion.47, f32[36,128,128]{2,1,0:T(8,128)} %bitcast.107), kind=kCustom, calls=%fused_computation.3.clone.1 | custom fusion | flops 589824 | bytes 7078032 | tf_op jit(solution)/shard_map/while/body/eval_jaxpr/scatter-add | solution.py:98
  344.5 1.1 reshape.302
  346.3 2.9 fusion.49
  349.9 4.2 fusion.51
  354.2 3.5 reshape.303
  357.6 1.7 copy.100
  359.4 9.6 %scatter_fusion = f32[32,128,128]{2,1,0:T(8,128)} fusion(f32[32,128,128]{2,1,0:T(8,128)} %get-tuple-element.276, s32[36]{0:T(128)S(1)} %fusion.47, f32[36,128,128]{2,1,0:T(8,128)} %bitcast.107), kind=kCustom, calls=%fused_computation.3.clone.1 | custom fusion | flops 589824 | bytes 7078032 | tf_op jit(solution)/shard_map/while/body/eval_jaxpr/scatter-add | solution.py:98
  375.6 2.9 fusion.49
  379.2 4.2 fusion.51
  383.5 3.5 reshape.303
  386.9 1.7 copy.100
  388.7 9.8 %scatter_fusion = f32[32,128,128]{2,1,0:T(8,128)} fusion(f32[32,128,128]{2,1,0:T(8,128)} %get-tuple-element.276, s32[36]{0:T(128)S(1)} %fusion.47, f32[36,128,128]{2,1,0:T(8,128)} %bitcast.107), kind=kCustom, calls=%fused_computation.3.clone.1 | custom fusion | flops 589824 | bytes 7078032 | tf_op jit(solution)/shard_map/while/body/eval_jaxpr/scatter-add | solution.py:98
  398.5 4.9 all-to-all-start.1
  404.2 1.5 fusion.21
  407.1 45.3 %all-to-all-done.1 = f32[16,2,128,128]{3,2,1,0:T(8,128)S(1)} async-done(((f32[16,2,128,128]{3,2,1,0:T(8,128)}), f32[16,2,128,128]{3,2,1,0:T(8,128)S(1)}, u32[]{:S(2)}, u32[]{:S(2)}) %all-to-all-start.1) | async-done | bytes 2097184 | tf_op jit(solution)/shard_map/all_to_all | solution.py:104
  452.4 2.7 scatter_fusion.1
  456.1 168.7 %reduce-scatter.2.cloned.1.call-done = f32[32,256]{1,0:T(8,128)} async-done(((f32[1024,256]{1,0:T(8,128)}), f32[32,256]{1,0:T(8,128)}) %reduce-scatter.2.cloned.1.call-update) | async-done | bytes 32784 | tf_op jit(solution)/shard_map/reduce_scatter | solution.py:124
  624.8 1.4 copy.66
  626.2 244.5 %all-gather.10.cloned.1.call-done = f32[512,128,128]{2,1,0:T(8,128)} async-done(((f32[16,128,128]{2,1,0:T(8,128)}), f32[512,128,128]{2,1,0:T(8,128)}) %all-gather.10.cloned.1.call-update) | async-done | bytes 33554448 | tf_op jit(solution)/shard_map/all_gather | solution.py:12
  870.7 12.7 %reduce_sum.18 = f32[16,128,128]{2,1,0:T(8,128)} reduce(f32[32,16,128,128]{3,2,1,0:T(8,128)} %bitcast.111, f32[]{:T(128)} %constant.32.clone.1), dimensions={0}, to_apply=%region_5.6 | reduce | flops 8126464 | bytes 34603012 | tf_op jit(solution)/shard_map/reduce_sum | solution.py:13
  (231 shorter events, 52.4 us)
Async XLA Ops:
  7.2 87.9 %all-gather.8.cloned.1.call-start = ((), (), s32[]{:S(2)}) async-start(), calls=%async_computation.5 | async-start | bytes 1081344 | tf_op jit(solution)/shard_map/all_gather | solution.py:54
  8.6 149.0 %all-gather.6.cloned.1.call-start = ((), (), s32[]{:S(2)}) async-start(), calls=%async_computation.3 | async-start | bytes 8912896 | tf_op jit(solution)/shard_map/all_gather | solution.py:61
  10.7 387.8 %all-to-all-start = ((s32[16,1,2]{2,1,0:T(1,128)}), s32[16,1,2]{2,1,0:T(1,128)S(1)}, u32[]{:S(2)}, u32[]{:S(2)}) async-start(s32[16,1,2]{2,1,0:T(1,128)} %copy.56), calls=%async_computation | async-start | bytes 16384 | tf_op jit(solution)/shard_map/all_to_all | solution.py:57
  163.4 3.8 copy-start
  183.1 9.7 %copy-start.1 = (bf16[32,128,128]{2,1,0:T(8,128)(2,1)S(1)}, bf16[32,128,128]{2,1,0:T(8,128)(2,1)}, u32[]{:S(2)}) copy-start(bf16[32,128,128]{2,1,0:T(8,128)(2,1)} %copy-done) | copy-start | bytes 3145732 | tf_op jit(solution)/shard_map/while
  192.8 3.8 copy-start
  212.5 9.7 %copy-start.1 = (bf16[32,128,128]{2,1,0:T(8,128)(2,1)S(1)}, bf16[32,128,128]{2,1,0:T(8,128)(2,1)}, u32[]{:S(2)}) copy-start(bf16[32,128,128]{2,1,0:T(8,128)(2,1)} %copy-done) | copy-start | bytes 3145732 | tf_op jit(solution)/shard_map/while
  222.2 3.8 copy-start
  241.9 9.7 %copy-start.1 = (bf16[32,128,128]{2,1,0:T(8,128)(2,1)S(1)}, bf16[32,128,128]{2,1,0:T(8,128)(2,1)}, u32[]{:S(2)}) copy-start(bf16[32,128,128]{2,1,0:T(8,128)(2,1)} %copy-done) | copy-start | bytes 3145732 | tf_op jit(solution)/shard_map/while
  251.7 3.8 copy-start
  271.4 9.6 %copy-start.1 = (bf16[32,128,128]{2,1,0:T(8,128)(2,1)S(1)}, bf16[32,128,128]{2,1,0:T(8,128)(2,1)}, u32[]{:S(2)}) copy-start(bf16[32,128,128]{2,1,0:T(8,128)(2,1)} %copy-done) | copy-start | bytes 3145732 | tf_op jit(solution)/shard_map/while
  281.0 3.8 copy-start
  300.7 9.6 %copy-start.1 = (bf16[32,128,128]{2,1,0:T(8,128)(2,1)S(1)}, bf16[32,128,128]{2,1,0:T(8,128)(2,1)}, u32[]{:S(2)}) copy-start(bf16[32,128,128]{2,1,0:T(8,128)(2,1)} %copy-done) | copy-start | bytes 3145732 | tf_op jit(solution)/shard_map/while
  310.3 3.8 copy-start
  330.0 9.7 %copy-start.1 = (bf16[32,128,128]{2,1,0:T(8,128)(2,1)S(1)}, bf16[32,128,128]{2,1,0:T(8,128)(2,1)}, u32[]{:S(2)}) copy-start(bf16[32,128,128]{2,1,0:T(8,128)(2,1)} %copy-done) | copy-start | bytes 3145732 | tf_op jit(solution)/shard_map/while
  339.7 3.8 copy-start
  359.4 9.6 %copy-start.1 = (bf16[32,128,128]{2,1,0:T(8,128)(2,1)S(1)}, bf16[32,128,128]{2,1,0:T(8,128)(2,1)}, u32[]{:S(2)}) copy-start(bf16[32,128,128]{2,1,0:T(8,128)(2,1)} %copy-done) | copy-start | bytes 3145732 | tf_op jit(solution)/shard_map/while
  369.0 3.8 copy-start
  388.7 9.8 %copy-start.1 = (bf16[32,128,128]{2,1,0:T(8,128)(2,1)S(1)}, bf16[32,128,128]{2,1,0:T(8,128)(2,1)}, u32[]{:S(2)}) copy-start(bf16[32,128,128]{2,1,0:T(8,128)(2,1)} %copy-done) | copy-start | bytes 3145732 | tf_op jit(solution)/shard_map/while
  398.5 53.8 %all-to-all-start.1 = ((f32[16,2,128,128]{3,2,1,0:T(8,128)}), f32[16,2,128,128]{3,2,1,0:T(8,128)S(1)}, u32[]{:S(2)}, u32[]{:S(2)}) async-start(f32[16,2,128,128]{3,2,1,0:T(8,128)} %bitcast.109), calls=%async_computation.1 | async-start | bytes 4194304 | tf_op jit(solution)/shard_map/all_to_all | solution.py:104
  403.4 221.4 %reduce-scatter.2.cloned.1.call-start = ((), (), s32[]{:S(2)}) async-start(), calls=%async_computation.4 | async-start | bytes 1081344 | tf_op jit(solution)/shard_map/reduce_scatter | solution.py:124
  405.7 465.0 %all-gather.10.cloned.1.call-start = ((), (), s32[]{:S(2)}) async-start(), calls=%async_computation.6 | async-start | bytes 34603008 | tf_op jit(solution)/shard_map/all_gather | solution.py:12
  455.1 1.0 copy-start.2
Sparse Core Ops, SparseCore 0:
  11.7 83.2 all-gather.7
  97.2 60.3 all-gather.5
  408.6 216.1 reduce-scatter.1
  628.4 242.2 all-gather.9
